TPU v7x, 128 devices: a whole 4x4x4 slice. The times are simulated.
128 devices in a mesh: src: 16 (over y, z), win: 8 (over x, core).
Axes of the slice: x: 4, y: 4, z: 4, core: 2. Of those that a mesh axis runs over, the one named last changes fastest.
Arguments:
- src_design: float32 [65536, 5, 128], P(('src', 'win')), may hold values from -6 to 6
- att_comp: float32 [65536, 4, 128], P(('src', 'win')), may hold values from -6 to 6
- spline_phase: float32 [65536, 128], P(('src', 'win')), may hold values from 0 to 1
- knot_offset: int32 [65536, 128], P(('src', 'win')), may hold values from 0 to 60
- obs_weight: float32 [65536, 128], P(('src', 'win')), may hold values from 9.765625e-05 to 0.0009765625
- residual: float32 [65536, 128], P(('src', 'win')), may hold values from -220 to 220
- block_source: int32 [65536], P(('src', 'win')), may hold values from 0 to 4095, as said below
- block_window: int32 [65536], P(('src', 'win')), may hold values from 0 to 255, as said below
- send_list: int32 [2048, 64], P(('src', 'win')), may hold values from 0 to 511, as said below
- send_count: int32 [2048], P(('src', 'win')), may hold values from 0 to 64, as said below
Outputs:
- source_step: float32 [5, 4096], P(None, 'src')
- attitude_step: float32 [256, 256], P(('src', 'win'))
- final_residual: float32 [65536, 128], P(('src', 'win'))
Inputs may be any that keep to these rules, and one draw needn't show every extreme that they name: `block_source`: Non-decreasing along the blocks of each device; the device at src index i names only sources i * 256 to (i + 1) * 256 - 1. `block_window`: window W is owned by the device whose flat index in src+win order is W // 2; every block names a window owned by a device of its own win index. `send_list`: row k of a device's lists names, in increasing order and as indices 0 to 511 into that device's blocks, its blocks whose windows the device at src index k of its win column owns; every block is named exactly once among the valid entries; entries past the count are 0. `send_count`: the counts of one device sum to 512; in every draw some owner of each win column receives exactly 64 blocks from every device of that column.
All inputs are finite; a program needn't handle non-finite values.
Results may differ from a plain program's by a relative error of at most 0.0003.
Values sent between devices are 32-bit elements; how exact they have to be, the bound alone decides.
No kernel may reach another device: no remote copies, remote signals or barrier semaphores. Data moves between devices by JAX's collectives and lax.ppermute only.
A program may use at most 192 MiB of HBM per device.

v0:
```python
import jax
import jax.numpy as jnp
from jax import lax
from jax.sharding import PartitionSpec as P

OBS = 128
KNOTS = 64
WIN_SUB = 2
BLK_DEV = 512
SRC_DEV = 256


def spline_weights(phase):
    square = phase * phase
    cube = square * phase
    rest = 1.0 - phase
    return [
        rest * rest * rest / 6.0,
        (3.0 * cube - 6.0 * square + 4.0) / 6.0,
        (-3.0 * cube + 3.0 * square + 3.0 * phase + 1.0) / 6.0,
        cube / 6.0,
    ]


def group_terms(phase, comps, weight, resid_one):
    count = phase.shape[0]
    spline = spline_weights(phase)
    pairs = (comps[:, :, None, :] * comps[:, None, :, :]).reshape(count, 16, OBS)
    weighted_pairs = weight[:, None, :] * pairs
    products = []
    for spacing in range(4):
        for first in range(4 - spacing):
            products.append(spline[first] * spline[first + spacing])
    spline_pairs = jnp.stack(products, axis=1)
    pair_terms = (spline_pairs[:, :, None, :] * weighted_pairs[:, None, :, :]).reshape(
        count, 160, OBS
    )
    weighted_resid = weight * resid_one
    spline_all = jnp.stack(spline, axis=1) * weighted_resid[:, None, :]
    right_terms = (spline_all[:, :, None, :] * comps[:, None, :, :]).reshape(count, 16, OBS)
    return (pair_terms, right_terms)


def shift_knots(values, amount):
    if amount == 0:
        return values
    padding = jnp.zeros_like(values[:, :, :amount])
    return jnp.concatenate([padding, values[:, :, :-amount]], axis=2)


def fold_bands(totals):
    count = totals.shape[0]
    totals = totals.reshape(count, 176, KNOTS)
    pieces = []
    slot_index = 0
    for spacing in range(4):
        band = jnp.zeros((count, 16, KNOTS), jnp.float32)
        for first in range(4 - spacing):
            band = band + shift_knots(totals[:, slot_index * 16 : (slot_index + 1) * 16], first)
            slot_index += 1
        pieces.append(band)
    right = jnp.zeros((count, 4, KNOTS), jnp.float32)
    for first in range(4):
        right = right + shift_knots(totals[:, 160 + first * 4 : 164 + first * 4], first)
    pieces.append(right)
    return jnp.concatenate(pieces, axis=1).reshape(count, 68 * KNOTS)


def solve_folded(folded, prior):
    count = folded.shape[0]
    folded = folded.reshape(count, 68, KNOTS).transpose(0, 2, 1)
    bands = [
        folded[:, :, spacing * 16 : (spacing + 1) * 16].reshape(count, KNOTS, 4, 4)
        for spacing in range(4)
    ]
    right = folded[:, :, 64:68].reshape(count, KNOTS * 4)
    dense = jnp.zeros((count, KNOTS, 4, KNOTS, 4), jnp.float32)
    for spacing in range(4):
        stepper = jnp.eye(KNOTS, k=spacing, dtype=jnp.float32)
        dense = dense + bands[spacing][:, :, :, None, :] * stepper[None, :, None, :, None]
        if spacing > 0:
            dense = (
                dense
                + bands[spacing].transpose(0, 3, 1, 2)[:, None] * stepper.T[None, :, None, :, None]
            )
    normal = (
        dense.reshape(count, KNOTS * 4, KNOTS * 4)
        + prior * jnp.eye(KNOTS * 4, dtype=jnp.float32)[None]
    )
    factor = jnp.linalg.cholesky(normal)
    return jax.scipy.linalg.cho_solve((factor, True), right[:, :, None])[:, :, 0]


def source_stats(design, weight, resid):
    weighted = design * weight[:, None, :]
    cross = jnp.einsum("bpo,bqo->bpq", weighted, design, precision=lax.Precision.HIGHEST)
    right = jnp.einsum("bpo,bo->bp", weighted, resid, precision=lax.Precision.HIGHEST)
    return jnp.concatenate([cross.reshape(design.shape[0], 25), right], axis=1)


def solve_five(totals):
    factor = {}
    for across in range(5):
        for within in range(across + 1):
            entry = totals[across * 5 + within]
            if across == within:
                entry = entry + 1.0
            for before in range(within):
                entry = entry - factor[across, before] * factor[within, before]
            if across == within:
                factor[across, within] = jnp.sqrt(entry)
            else:
                factor[across, within] = entry / factor[within, within]
    forward = []
    for across in range(5):
        entry = totals[25 + across]
        for before in range(across):
            entry = entry - factor[across, before] * forward[before]
        forward.append(entry / factor[across, across])
    backward = [None] * 5
    for across in range(4, -1, -1):
        entry = forward[across]
        for later in range(across + 1, 5):
            entry = entry - factor[later, across] * backward[later]
        backward[across] = entry / factor[across, across]
    return jnp.stack(backward, axis=0)


def owner_partials(phase, comps, weight, resid_one, knots, subs):
    count = phase.shape[0]
    group = min(64, count)
    turns = count // group
    columns = WIN_SUB * KNOTS

    def one_group(carry, pieces):
        phase_g, comps_g, weight_g, resid_g, knots_g, subs_g = pieces
        pair_terms, right_terms = group_terms(phase_g, comps_g, weight_g, resid_g)
        target = subs_g[:, None] * KNOTS + knots_g
        target_hot = (target[:, :, None] == jnp.arange(columns)[None, None, :]).astype(jnp.float32)
        pair_sum = jnp.einsum(
            "gfo,goj->fj", pair_terms, target_hot, precision=lax.Precision.HIGHEST
        )
        right_sum = jnp.einsum(
            "gfo,goj->fj", right_terms, target_hot, precision=lax.Precision.HIGHEST
        )
        return ((carry[0] + pair_sum, carry[1] + right_sum), None)

    pieces = (
        phase.reshape(turns, group, OBS),
        comps.reshape(turns, group, 4, OBS),
        weight.reshape(turns, group, OBS),
        resid_one.reshape(turns, group, OBS),
        knots.reshape(turns, group, OBS),
        subs.reshape(turns, group),
    )
    start = (jnp.zeros((160, columns), jnp.float32), jnp.zeros((16, columns), jnp.float32))
    sums, unused = lax.scan(one_group, start, pieces)
    joined = jnp.concatenate([sums[0], sums[1]], axis=0).reshape(176, WIN_SUB, KNOTS)
    return joined.transpose(1, 0, 2).reshape(WIN_SUB, 176 * KNOTS)


def attitude_correction(panel_rows, knots, phase, comps):
    count = panel_rows.shape[0]
    grid = jnp.concatenate(
        [panel_rows.reshape(count, KNOTS, 4), jnp.zeros((count, 3, 4), jnp.float32)], axis=1
    )
    stacked = jnp.concatenate([grid[:, first : first + KNOTS] for first in range(4)], axis=2)
    knot_hot = (knots[:, :, None] == jnp.arange(KNOTS)[None, None, :]).astype(jnp.float32)
    picked = jnp.einsum("boj,bjf->bfo", knot_hot, stacked, precision=lax.Precision.HIGHEST)
    spline = spline_weights(phase)
    correction = jnp.zeros_like(phase)
    for first in range(4):
        summed = jnp.sum(comps * picked[:, first * 4 : first * 4 + 4], axis=1)
        correction = correction + spline[first] * summed
    return correction


def shards(
    src_design,
    att_comp,
    spline_phase,
    knot_offset,
    obs_weight,
    residual,
    block_source,
    block_window,
    send_list,
    send_count,
):
    n_win = lax.axis_size("win")
    capacity = send_list.shape[1]
    owners = send_list.shape[0]
    local_source = block_source - lax.axis_index("src") * SRC_DEV
    source_hot = (local_source[:, None] == jnp.arange(SRC_DEV)[None, :]).astype(jnp.float32)
    stats = source_stats(src_design, obs_weight, residual)
    totals = jnp.einsum("bf,bs->fs", stats, source_hot, precision=lax.Precision.HIGHEST)
    totals = lax.psum(totals, "win")
    source_step = solve_five(totals)
    per_block = jnp.einsum("fs,bs->bf", source_step, source_hot, precision=lax.Precision.HIGHEST)
    resid_one = residual - jnp.sum(src_design * per_block[:, :, None], axis=1)
    column_window = block_window // (n_win * WIN_SUB) * WIN_SUB + block_window % WIN_SUB
    obs_src = OBS * BLK_DEV * n_win // SRC_DEV
    obs_win = OBS * BLK_DEV // WIN_SUB
    prior = 0.005 * obs_win / obs_src
    slot_valid = jnp.arange(capacity)[None, :] < send_count[:, None]
    flat_list = send_list.reshape(-1)
    valid_flat = slot_valid.reshape(-1)
    valid_weight = obs_weight[flat_list] * valid_flat.astype(jnp.float32)[:, None]
    payload = jnp.concatenate(
        [
            spline_phase[flat_list][:, None],
            valid_weight[:, None],
            resid_one[flat_list][:, None],
            att_comp[flat_list],
        ],
        axis=1,
    )
    payload = payload.reshape(owners, capacity, 7, OBS)
    knots_out = knot_offset[flat_list].reshape(owners, capacity, OBS)
    subs_out = (block_window[flat_list] % WIN_SUB).reshape(owners, capacity)
    got_payload, got_knots, got_subs = (
        lax.all_to_all(payload, "src", split_axis=0, concat_axis=0, tiled=True),
        lax.all_to_all(knots_out, "src", split_axis=0, concat_axis=0, tiled=True),
        lax.all_to_all(subs_out, "src", split_axis=0, concat_axis=0, tiled=True),
    )
    got_payload = got_payload.reshape(owners * capacity, 7, OBS)
    got_knots = got_knots.reshape(owners * capacity, OBS)
    totals_att = owner_partials(
        got_payload[:, 0],
        got_payload[:, 3:7],
        got_payload[:, 1],
        got_payload[:, 2],
        got_knots,
        got_subs.reshape(-1),
    )
    attitude_step = solve_folded(fold_bands(totals_att), prior)
    panels = lax.all_gather(attitude_step, "src", axis=0, tiled=True)
    panel_rows = panels[column_window]
    correction = attitude_correction(panel_rows, knot_offset, spline_phase, att_comp)
    return (source_step, attitude_step, resid_one - correction)


def solution(mesh):
    return jax.shard_map(
        shards,
        mesh=mesh,
        in_specs=(
            P(("src", "win"), None, None),
            P(("src", "win"), None, None),
            P(("src", "win"), None),
            P(("src", "win"), None),
            P(("src", "win"), None),
            P(("src", "win"), None),
            P(("src", "win")),
            P(("src", "win")),
            P(("src", "win"), None),
            P(("src", "win")),
        ),
        out_specs=(P(None, "src"), P(("src", "win"), None), P(("src", "win"), None)),
        check_vma=False,
    )
```

profile of v0, /device:TPU:0, one launch (start us, length us, event | category | flops | bytes accessed | tf_op | source)
XLA Modules:
  0.0 787.5 jit_solution(14933603180917023108)
XLA Ops:
  1.5 6.3 gather_fusion.4
  8.5 8.2 %all-to-all-start.1 = ((s32[16,1,64]{2,1,0:T(1,128)}), s32[16,1,64]{2,1,0:T(1,128)}, u32[]{:S(2)}, u32[]{:S(2)}) async-start(s32[16,1,64]{2,1,0:T(1,128)} %and_select_fusion), calls=%async_computation.1 | async-start | bytes 16384 | tf_op jit(solution)/shard_map/all_to_all | solution.py:224
  16.7 4.0 gather_fusion.1
  20.8 6.2 fusion.30
  29.0 4.0 fusion.28
  33.6 25.9 %psum.7 = f32[30,256]{1,0:T(8,128)S(1)} all-reduce(f32[30,256]{1,0:T(8,128)S(1)} %fusion.39), channel_id=1, replica_groups=mesh['src'=16,'win'=8] {'win'}, use_global_device_ids=true, to_apply=%region_0.0 | all-reduce | flops 7680 | bytes 61440 | tf_op jit(solution)/shard_map/psum | solution.py:197
  63.5 7.9 %gather_fusion.3 = f32[1024,4,128]{2,1,0:T(4,128)} fusion(f32[512,4,128]{2,1,0:T(4,128)S(1)} %copy-done.8, s32[1024]{0:T(1024)S(1)} %broadcast_clamp_fusion), kind=kCustom, calls=%fused_computation.3 | custom fusion | bytes 4198400 | tf_op jit(solution)/shard_map/gather | solution.py:214
  73.3 4.0 gather_fusion
  82.2 7.0 all-to-all-start
  89.3 4.0 gather_fusion.5
  93.4 3.8 mul.1113
  97.2 8.3 %mul.1114 = f32[256,256]{1,0:T(8,128)S(1)} reshape(f32[64,4,64,4]{3,2,1,0:T(8,128)} %mul.1113) | data formatting | bytes 524288 | tf_op jit(solution)/shard_map/mul | solution.py:80
  106.4 3.8 mul.1119
  110.2 8.3 %mul.1120 = f32[256,256]{1,0:T(8,128)S(1)} reshape(f32[64,4,64,4]{3,2,1,0:T(8,128)} %mul.1119) | data formatting | bytes 524288 | tf_op jit(solution)/shard_map/mul | solution.py:84
  119.4 3.8 mul.1126
  123.3 8.3 %mul.1127 = f32[256,256]{1,0:T(8,128)S(1)} reshape(f32[64,4,64,4]{3,2,1,0:T(8,128)} %mul.1126) | data formatting | bytes 524288 | tf_op jit(solution)/shard_map/mul | solution.py:80
  132.4 3.8 mul.1132
  136.2 8.3 %mul.1133 = f32[256,256]{1,0:T(8,128)S(1)} reshape(f32[64,4,64,4]{3,2,1,0:T(8,128)} %mul.1132) | data formatting | bytes 524288 | tf_op jit(solution)/shard_map/mul | solution.py:84
  145.5 3.8 mul.1139
  149.3 8.3 %mul.1140 = f32[256,256]{1,0:T(8,128)S(1)} reshape(f32[64,4,64,4]{3,2,1,0:T(8,128)} %mul.1139) | data formatting | bytes 524288 | tf_op jit(solution)/shard_map/mul | solution.py:80
  158.4 3.8 mul.1145
  162.2 19.5 %mul.1146 = f32[256,256]{1,0:T(8,128)S(1)} reshape(f32[64,4,64,4]{3,2,1,0:T(8,128)} %mul.1145) | data formatting | bytes 524288 | tf_op jit(solution)/shard_map/mul | solution.py:84
  182.6 3.8 mul.1106
  186.5 8.3 %mul.1107 = f32[256,256]{1,0:T(8,128)S(1)} reshape(f32[64,4,64,4]{3,2,1,0:T(8,128)} %mul.1106) | data formatting | bytes 524288 | tf_op jit(solution)/shard_map/mul | solution.py:80
  196.9 7.2 all-to-all-start.2
  209.2 5.1 all-to-all-done.2
  214.3 250.8 %while.15 = (s32[]{:T(128)}, f32[160,128]{1,0:T(8,128)S(1)}, f32[16,128]{1,0:T(8,128)}, f32[16,64,128]{2,1,0:T(8,128)S(1)}, f32[16,64,128]{2,1,0:T(8,128)}, /*in...) while((s32[]{:T(128)}, f32[160,128]{1,0:T(8,128)S(1)}, ...), condition=%wide.region_3.4_spmd.clone, body=%wide.region_2.3_spmd.clone.sunk | while | flops 2218856448 | bytes 17449884 | solution.py:157
  221.3 5.6 fusion.158
  236.3 5.6 fusion.158
  252.0 5.6 fusion.158
  267.7 5.6 fusion.158
  283.5 5.6 fusion.158
  299.2 5.6 fusion.158
  314.9 5.6 fusion.158
  330.6 5.6 fusion.158
  346.3 5.6 fusion.158
  362.0 5.6 fusion.158
  377.8 5.6 fusion.158
  393.5 5.6 fusion.158
  409.2 5.6 fusion.158
  424.9 5.6 fusion.158
  440.6 5.6 fusion.158
  456.4 5.6 fusion.158
  468.0 6.8 mul.1104
  474.9 15.0 %mul.1105 = f32[2,256,256]{2,1,0:T(8,128)S(1)} reshape(f32[2,64,4,64,4]{4,3,2,1,0:T(8,128)} %mul.1104) | data formatting | bytes 1048576 | tf_op jit(solution)/shard_map/mul | solution.py:80
  490.4 6.8 mul.1111
  497.2 15.4 %mul.1112 = f32[2,256,256]{2,1,0:T(8,128)S(1)} reshape(f32[2,64,4,64,4]{4,3,2,1,0:T(8,128)} %mul.1111) | data formatting | bytes 1048576 | tf_op jit(solution)/shard_map/mul | solution.py:80
  513.0 7.9 %mul.1117 = f32[2,64,4,64,4]{4,3,2,1,0:T(8,128)} broadcast(f32[2,4,64,4]{3,2,1,0:T(8,128)S(1)} %copy.457), dimensions={0,2,3,4} | broadcast | bytes 532480 | tf_op jit(solution)/shard_map/mul | solution.py:84
  520.9 15.0 %mul.1118 = f32[2,256,256]{2,1,0:T(8,128)S(1)} reshape(f32[2,64,4,64,4]{4,3,2,1,0:T(8,128)} %mul.1117) | data formatting | bytes 1048576 | tf_op jit(solution)/shard_map/mul | solution.py:84
  536.4 6.8 mul.1124
  543.2 15.0 %mul.1125 = f32[2,256,256]{2,1,0:T(8,128)S(1)} reshape(f32[2,64,4,64,4]{4,3,2,1,0:T(8,128)} %mul.1124) | data formatting | bytes 1048576 | tf_op jit(solution)/shard_map/mul | solution.py:80
  558.6 7.9 %mul.1130 = f32[2,64,4,64,4]{4,3,2,1,0:T(8,128)} broadcast(f32[2,4,64,4]{3,2,1,0:T(8,128)S(1)} %copy.464), dimensions={0,2,3,4} | broadcast | bytes 532480 | tf_op jit(solution)/shard_map/mul | solution.py:84
  566.5 15.2 %mul.1131 = f32[2,256,256]{2,1,0:T(8,128)S(1)} reshape(f32[2,64,4,64,4]{4,3,2,1,0:T(8,128)} %mul.1130) | data formatting | bytes 1048576 | tf_op jit(solution)/shard_map/mul | solution.py:84
  583.0 6.8 mul.1137
  589.8 15.0 %mul.1138 = f32[2,256,256]{2,1,0:T(8,128)S(1)} reshape(f32[2,64,4,64,4]{4,3,2,1,0:T(8,128)} %mul.1137) | data formatting | bytes 1048576 | tf_op jit(solution)/shard_map/mul | solution.py:80
  606.0 7.9 %mul.1143 = f32[2,64,4,64,4]{4,3,2,1,0:T(8,128)} broadcast(f32[2,4,64,4]{3,2,1,0:T(8,128)S(1)} %copy.471), dimensions={0,2,3,4} | broadcast | bytes 532480 | tf_op jit(solution)/shard_map/mul | solution.py:84
  613.9 15.0 %mul.1144 = f32[2,256,256]{2,1,0:T(8,128)S(1)} reshape(f32[2,64,4,64,4]{4,3,2,1,0:T(8,128)} %mul.1143) | data formatting | bytes 1048576 | tf_op jit(solution)/shard_map/mul | solution.py:84
  632.5 23.5 %custom-call.20 = f32[2,128,128]{2,1,0:T(8,128)S(1)} custom-call(f32[2,128,128]{2,1,0:T(8,128)S(1)} %cholesky.122), custom_call_target="Cholesky" | custom-call | tf_op jit(solution)/shard_map/jit(cholesky)/cholesky | solution.py:90
  656.0 19.9 %custom-call.21 = f32[2,1,128,128]{2,3,1,0:T(8,128)S(1)} custom-call(f32[2,1,128,128]{3,2,1,0:T(8,128)S(1)} %select_bitcast_fusion), custom_call_target="InvertDiagBlocksLowerTriangular" | custom-call | tf_op jit(solution)/shard_map/jit(cholesky)/cholesky | solution.py:90
  676.5 23.5 %custom-call.22 = f32[2,128,128]{2,1,0:T(8,128)S(1)} custom-call(f32[2,128,128]{2,1,0:T(8,128)S(1)} %convolution_subtract_fusion), custom_call_target="Cholesky" | custom-call | tf_op jit(solution)/shard_map/jit(cholesky)/cholesky | solution.py:90
  700.4 5.1 while.14
  705.5 40.1 %custom-call.23 = f32[2,2,128,128]{2,3,1,0:T(8,128)S(1)} custom-call(f32[2,2,128,128]{3,2,1,0:T(8,128)} %bitcast.261), custom_call_target="InvertDiagBlocksLowerTriangular" | custom-call | tf_op jit(solution)/shard_map/jit(_cho_solve)/vmap()/triangular_solve | solution.py:91
  747.5 21.4 %all-gather = f32[32,256,1]{1,2,0:T(1,128)S(1)} all-gather(f32[2,256,1]{1,2,0:T(1,128)S(1)} %pad_maximum_fusion.2), channel_id=2, replica_groups=mesh['src'=16,'win'=8] {'src'}, dimensions={0}, use_global_device_ids=true | all-gather | bytes 34816 | tf_op jit(solution)/shard_map/all_gather | solution.py:237
  773.9 9.3 %fusion.19 = f32[512,16,128]{2,1,0:T(8,128)S(1)} fusion(s32[512,128]{1,0:T(8,128)S(1)} %copy-done.6, f32[512,64,4]{1,2,0:T(4,128)S(1)} %get-tuple-element.195, f32[512,64,4]{1,2,0:T(4,128)S(1)} %get-tuple-element.194, f32[512,64,4]{1,2,0:T(4,128)S(1)} %get-tuple-element.193, f32[512,64,4]{1,2,0:T(4,128)S(1)} %copy.480), kind=kOutput, calls=%fused_computation.57 | convolution fusion | flops 811073536 | bytes 6553600 | tf_op jit(solution)/shard_map/boj,bjf->bfo/dot_general | solution.py:169
  (526 shorter events, 214.1 us)
Async XLA Ops:
  0.6 16.0 %copy-start.5 = (f32[512,128]{1,0:T(8,128)S(1)}, f32[512,128]{1,0:T(8,128)}, u32[]{:S(2)}) copy-start(f32[512,128]{1,0:T(8,128)} %param.16) | copy-start | bytes 786436
  1.5 19.2 %copy-start.7 = (f32[512,5,128]{2,0,1:T(8,128)S(1)}, f32[512,5,128]{2,0,1:T(8,128)}, u32[]{:S(2)}) copy-start(f32[512,5,128]{2,0,1:T(8,128)} %param.12) | copy-start | bytes 3932164
  8.5 73.8 %all-to-all-start.1 = ((s32[16,1,64]{2,1,0:T(1,128)}), s32[16,1,64]{2,1,0:T(1,128)}, u32[]{:S(2)}, u32[]{:S(2)}) async-start(s32[16,1,64]{2,1,0:T(1,128)} %and_select_fusion), calls=%async_computation.1 | async-start | bytes 16384 | tf_op jit(solution)/shard_map/all_to_all | solution.py:224
  20.8 8.2 %copy-start.10 = (f32[512,128]{1,0:T(8,128)S(1)}, f32[512,128]{1,0:T(8,128)}, u32[]{:S(2)}) copy-start(f32[512,128]{1,0:T(8,128)} %param.17) | copy-start | bytes 786436
  27.0 6.2 copy-start.14
  59.5 4.0 copy-start.8
  59.6 0.6 copy-start.13
  60.7 10.8 %copy-start.1 = (f32[512,128]{1,0:T(8,128)}, f32[512,128]{1,0:T(8,128)S(1)}, u32[]{:S(2)}) copy-start(f32[512,128]{1,0:T(8,128)S(1)} %sub.412) | copy-start | bytes 786436
  63.5 9.7 %copy-start.15 = (s32[16]{0:T(128)S(1)}, s32[16]{0:T(128)}, u32[]{:S(2)}) copy-start(s32[16]{0:T(128)} %param.21) | copy-start | bytes 196
  63.5 9.8 %copy-start.3 = (f32[512,128]{1,0:T(8,128)S(1)}, f32[512,128]{1,0:T(8,128)}, u32[]{:S(2)}) copy-start(f32[512,128]{1,0:T(8,128)} %param.14) | copy-start | bytes 786436
  82.2 7.1 copy-start.6
  82.2 114.7 %all-to-all-start = ((f32[16,64,7,128]{3,1,2,0:T(8,128)}), f32[16,64,7,128]{3,1,2,0:T(8,128)}, u32[]{:S(2)}, u32[]{:S(2)}) async-start(f32[16,64,7,128]{3,1,2,0:T(8,128)} %copy.444), calls=%async_computation | async-start | bytes 7340032 | tf_op jit(solution)/shard_map/all_to_all | solution.py:222
  186.5 9.2 %copy-start = (s32[512]{0:T(512)S(1)}, s32[512]{0:T(512)}, u32[]{:S(2)}) copy-start(s32[512]{0:T(512)} %param.19) | copy-start | bytes 6148
  196.9 17.4 %all-to-all-start.2 = ((s32[16,64,128]{2,1,0:T(8,128)}), s32[16,64,128]{2,1,0:T(8,128)}, u32[]{:S(2)}, u32[]{:S(2)}) async-start(s32[16,64,128]{2,1,0:T(8,128)} %bitcast.13), calls=%async_computation.2 | async-start | bytes 1048576 | tf_op jit(solution)/shard_map/all_to_all | solution.py:223
  632.1 68.1 %copy-start.11 = (pred[256,256]{1,0:T(8,128)(4,1)S(1)}, pred[256,256]{1,0:T(8,128)(4,1)}, u32[]{:S(2)}) copy-start(pred[256,256]{1,0:T(8,128)(4,1)} %iota_compare_fusion.17) | copy-start | bytes 196612
  632.1 68.2 %copy-start.16 = (s32[2]{0:T(128)S(1)}, s32[2]{0:T(128)}, u32[]{:S(2)}) copy-start(s32[2]{0:T(128)} %iota_multiply_fusion) | copy-start | bytes 28
  632.4 137.1 %copy-start.12 = (s32[1024]{0:T(1024)S(1)}, s32[1024]{0:T(1024)}, u32[]{:S(2)}) copy-start(s32[1024]{0:T(1024)} %pad_clamp_fusion) | copy-start | bytes 12292
  773.9 9.4 %copy-start.9 = (f32[512,4,128]{2,1,0:T(4,128)S(1)}, f32[512,4,128]{2,1,0:T(4,128)}, u32[]{:S(2)}) copy-start(f32[512,4,128]{2,1,0:T(4,128)} %param.13) | copy-start | bytes 3145732
  783.2 3.1 copy-start.2
  783.2 3.1 copy-start.4
where the time goes:
time: 801 us; the launch traced here: 788 us
  local copies, waits for them, and re-layouts  336 us (42%)
  other arithmetic  212 us (26%)
  matrix products  161 us (20%)
  blocking collectives  47.2 us (6%)
  starting transfers between devices  22.5 us (3%)
    mul x28, local copies, waits for them, and re-layouts, solve_folded(): bands[spacing][:, :, :, None, :] * stepper[None, :, None, :, None]  142 us
    mul x18, local copies, waits for them, and re-layouts, solve_folded(): bands[spacing].transpose(0, 3, 1, 2)[:, None]  120 us
    dot_general x16, matrix products, one_group(): jnp.einsum('gfo,goj->fj', pair_terms, target_hot, precision=lax.Precision...  89.5 us
    another operation x9, other arithmetic, solve_folded(): factor = jnp.linalg.cholesky(normal)  67 us
    dot_general x16, matrix products, one_group(): jnp.einsum('gfo,goj->fj', right_terms, target_hot, precision=lax.Precisio...  49.1 us
    mul x16, other arithmetic, group_terms(): spline_pairs[:, :, None, :] * weighted_pairs[:, None, :, :]  48.5 us
    another operation x7, other arithmetic, solve_folded(): jax.scipy.linalg.cho_solve((factor, True), right[:, :, None])[:, :, 0]  41.5 us
    psum x1, blocking collectives, shards(): totals = lax.psum(totals, 'win')  25.9 us
  transfers between devices with their start and end apart: 3, of which 1 were waited for; matrix products, arithmetic and copies ran while one was open for 19% of the time, Pallas kernels for 0%

commit v1 on v0

--- a/solution.py
+++ b/solution.py
@@ -234,7 +234,12 @@
         got_subs.reshape(-1),
     )
     attitude_step = solve_folded(fold_bands(totals_att), prior)
-    panels = lax.all_gather(attitude_step, "src", axis=0, tiled=True)
+    ring = [attitude_step]
+    for hop in range(15):
+        ring.append(lax.ppermute(ring[-1], "src", [(dev, (dev + 1) % 16) for dev in range(16)]))
+    panels = jnp.roll(
+        jnp.concatenate(ring[::-1], axis=0), (lax.axis_index("src") + 1) * ring[0].shape[0], axis=0
+    )
     panel_rows = panels[column_window]
     correction = attitude_correction(panel_rows, knot_offset, spline_phase, att_comp)
     return (source_step, attitude_step, resid_one - correction)

time: 801 us -> 873 us (1.090)
  waiting for transfers between devices: 5.12 us -> 108 us
  blocking collectives: 47.2 us -> 25.7 us
  local copies, waits for them, and re-layouts: 336 us -> 325 us
    ppermute x0 -> x15, waiting for transfers between devices: none -> 103 us  [shards(): lax.ppermute(ring[-1], 'src', [(dev, (dev + 1) % 16) for dev in range(16)])]
    all_gather x1 -> x0, blocking collectives: 21.4 us -> none  [shards(): panels = lax.all_gather(attitude_step, 'src', axis=0, tiled=True)]
    mul x18, local copies, waits for them, and re-layouts: 120 us -> 110 us  [solve_folded(): bands[spacing].transpose(0, 3, 1, 2)[:, None]]
    another operation x7 -> x6, other arithmetic: 41.5 us -> 41.4 us  [solve_folded(): jax.scipy.linalg.cho_solve((factor, True), right[:, :, None])[:, :, 0]]
  transfers between devices with their start and end apart: 3 -> 18, of which waited for: 1 -> 16; matrix products, arithmetic and copies ran while one was open for 19% -> 16% of each run, Pallas kernels for 0% -> 0%
where the time goes in v1:
time: 873 us; the launch traced here: 859 us
  local copies, waits for them, and re-layouts  325 us (37%)
  other arithmetic  212 us (24%)
  matrix products  161 us (18%)
  waiting for transfers between devices  108 us (12%)
  blocking collectives  25.7 us (3%)
  starting transfers between devices  23.1 us (3%)
    mul x28, local copies, waits for them, and re-layouts, solve_folded(): bands[spacing][:, :, :, None, :] * stepper[None, :, None, :, None]  142 us
    mul x18, local copies, waits for them, and re-layouts, solve_folded(): bands[spacing].transpose(0, 3, 1, 2)[:, None]  110 us
    ppermute x15, waiting for transfers between devices, shards(): lax.ppermute(ring[-1], 'src', [(dev, (dev + 1) % 16) for dev in range(16)])  103 us
    dot_general x16, matrix products, one_group(): jnp.einsum('gfo,goj->fj', pair_terms, target_hot, precision=lax.Precision...  89.5 us
    another operation x9, other arithmetic, solve_folded(): factor = jnp.linalg.cholesky(normal)  67 us
    dot_general x16, matrix products, one_group(): jnp.einsum('gfo,goj->fj', right_terms, target_hot, precision=lax.Precisio...  49.1 us
    mul x16, other arithmetic, group_terms(): spline_pairs[:, :, None, :] * weighted_pairs[:, None, :, :]  49.1 us
    another operation x6, other arithmetic, solve_folded(): jax.scipy.linalg.cho_solve((factor, True), right[:, :, None])[:, :, 0]  41.4 us
  transfers between devices with their start and end apart: 18, of which 16 were waited for; matrix products, arithmetic and copies ran while one was open for 16% of the time, Pallas kernels for 0%

profile of v1, /device:TPU:0, one launch (start us, length us, event | category | flops | bytes accessed | tf_op | source)
XLA Modules:
  0.0 859.1 jit_solution(1361344406044917600)
XLA Ops:
  1.5 6.3 gather_fusion.4
  8.5 8.2 all-to-all-start.1
  20.8 6.2 fusion.30
  33.6 25.7 %psum.7 = f32[30,256]{1,0:T(8,128)S(1)} all-reduce(f32[30,256]{1,0:T(8,128)S(1)} %fusion.39), channel_id=1, replica_groups=mesh['src'=16,'win'=8] {'win'}, use_global_device_ids=true, to_apply=%region_0.0 | all-reduce | flops 7680 | bytes 61440 | tf_op jit(solution)/shard_map/psum | solution.py:197
  63.4 8.0 gather_fusion.3
  82.1 7.0 all-to-all-start
  97.2 8.3 mul.1117
  110.2 8.3 mul.1123
  123.3 8.3 mul.1130
  136.3 8.3 mul.1136
  149.4 8.3 mul.1143
  162.4 8.7 %mul.1149 = f32[256,256]{1,0:T(8,128)S(1)} reshape(f32[64,4,64,4]{3,2,1,0:T(8,128)} %mul.1148) | data formatting | bytes 524288 | tf_op jit(solution)/shard_map/mul | solution.py:84
  175.8 8.3 mul.1110
  185.7 7.2 all-to-all-start.2
  203.1 251.5 %while.15 = (s32[]{:T(128)}, f32[160,128]{1,0:T(8,128)S(1)}, f32[16,128]{1,0:T(8,128)}, f32[16,64,128]{2,1,0:T(8,128)S(1)}, f32[16,64,128]{2,1,0:T(8,128)}, /*in...) while((s32[]{:T(128)}, f32[160,128]{1,0:T(8,128)S(1)}, ...), condition=%wide.region_3.4_spmd.clone, body=%wide.region_2.3_spmd.clone.sunk | while | flops 2218856448 | bytes 17449884 | solution.py:157
  210.1 5.6 fusion.160
  225.2 5.6 fusion.160
  240.9 5.6 fusion.160
  256.7 5.6 fusion.160
  272.5 5.6 fusion.160
  288.2 5.6 fusion.160
  304.0 5.6 fusion.160
  319.7 5.6 fusion.160
  335.5 5.6 fusion.160
  351.3 5.6 fusion.160
  367.0 5.6 fusion.160
  382.8 5.6 fusion.160
  398.6 5.6 fusion.160
  414.3 5.6 fusion.160
  430.1 5.6 fusion.160
  457.6 6.8 mul.1107
  464.4 15.0 %mul.1108 = f32[2,256,256]{2,1,0:T(8,128)S(1)} reshape(f32[2,64,4,64,4]{4,3,2,1,0:T(8,128)} %mul.1107) | data formatting | bytes 1048576 | tf_op jit(solution)/shard_map/mul | solution.py:80
  479.9 6.8 mul.1114
  486.7 15.2 %mul.1115 = f32[2,256,256]{2,1,0:T(8,128)S(1)} reshape(f32[2,64,4,64,4]{4,3,2,1,0:T(8,128)} %mul.1114) | data formatting | bytes 1048576 | tf_op jit(solution)/shard_map/mul | solution.py:80
  502.2 7.9 mul.1120
  510.1 15.0 %mul.1121 = f32[2,256,256]{2,1,0:T(8,128)S(1)} reshape(f32[2,64,4,64,4]{4,3,2,1,0:T(8,128)} %mul.1120) | data formatting | bytes 1048576 | tf_op jit(solution)/shard_map/mul | solution.py:84
  525.6 6.8 mul.1127
  532.4 15.0 %mul.1128 = f32[2,256,256]{2,1,0:T(8,128)S(1)} reshape(f32[2,64,4,64,4]{4,3,2,1,0:T(8,128)} %mul.1127) | data formatting | bytes 1048576 | tf_op jit(solution)/shard_map/mul | solution.py:80
  547.8 7.9 mul.1133
  555.7 15.4 %mul.1134 = f32[2,256,256]{2,1,0:T(8,128)S(1)} reshape(f32[2,64,4,64,4]{4,3,2,1,0:T(8,128)} %mul.1133) | data formatting | bytes 1048576 | tf_op jit(solution)/shard_map/mul | solution.py:84
  572.5 6.8 mul.1140
  579.3 15.0 %mul.1141 = f32[2,256,256]{2,1,0:T(8,128)S(1)} reshape(f32[2,64,4,64,4]{4,3,2,1,0:T(8,128)} %mul.1140) | data formatting | bytes 1048576 | tf_op jit(solution)/shard_map/mul | solution.py:80
  595.5 7.9 mul.1146
  603.4 15.0 %mul.1147 = f32[2,256,256]{2,1,0:T(8,128)S(1)} reshape(f32[2,64,4,64,4]{4,3,2,1,0:T(8,128)} %mul.1146) | data formatting | bytes 1048576 | tf_op jit(solution)/shard_map/mul | solution.py:84
  621.9 23.5 %custom-call.20 = f32[2,128,128]{2,1,0:T(8,128)S(1)} custom-call(f32[2,128,128]{2,1,0:T(8,128)S(1)} %cholesky.122), custom_call_target="Cholesky" | custom-call | tf_op jit(solution)/shard_map/jit(cholesky)/cholesky | solution.py:90
  645.5 19.8 %custom-call.21 = f32[2,1,128,128]{2,3,1,0:T(8,128)S(1)} custom-call(f32[2,1,128,128]{3,2,1,0:T(8,128)S(1)} %select_bitcast_fusion), custom_call_target="InvertDiagBlocksLowerTriangular" | custom-call | tf_op jit(solution)/shard_map/jit(cholesky)/cholesky | solution.py:90
  666.0 23.5 %custom-call.22 = f32[2,128,128]{2,1,0:T(8,128)S(1)} custom-call(f32[2,128,128]{2,1,0:T(8,128)S(1)} %convolution_subtract_fusion), custom_call_target="Cholesky" | custom-call | tf_op jit(solution)/shard_map/jit(cholesky)/cholesky | solution.py:90
  695.0 40.1 %custom-call.23 = f32[2,2,128,128]{2,3,1,0:T(8,128)S(1)} custom-call(f32[2,2,128,128]{3,2,1,0:T(8,128)} %bitcast.255), custom_call_target="InvertDiagBlocksLowerTriangular" | custom-call | tf_op jit(solution)/shard_map/jit(_cho_solve)/vmap()/triangular_solve | solution.py:91
  737.6 6.3 collective-permute-done
  744.0 6.9 collective-permute-done.1
  750.9 6.9 collective-permute-done.2
  757.8 6.9 collective-permute-done.3
  764.7 6.9 collective-permute-done.4
  771.6 6.9 collective-permute-done.5
  778.5 6.9 collective-permute-done.6
  785.4 6.9 collective-permute-done.7
  792.3 6.9 collective-permute-done.8
  799.2 6.9 collective-permute-done.9
  806.1 6.9 collective-permute-done.10
  813.0 6.9 collective-permute-done.11
  819.9 6.9 collective-permute-done.12
  826.8 6.9 collective-permute-done.13
  833.8 6.9 collective-permute-done.14
  845.1 9.3 %fusion.19 = f32[512,16,128]{2,1,0:T(8,128)S(1)} fusion(s32[512,128]{1,0:T(8,128)S(1)} %copy-done.6, f32[512,64,4]{1,2,0:T(4,128)S(1)} %get-tuple-element.195, f32[512,64,4]{1,2,0:T(4,128)S(1)} %get-tuple-element.194, f32[512,64,4]{1,2,0:T(4,128)S(1)} %get-tuple-element.193, f32[512,64,4]{1,2,0:T(4,128)S(1)} %copy.480), kind=kOutput, calls=%fused_computation.57 | convolution fusion | flops 811073536 | bytes 6553600 | tf_op jit(solution)/shard_map/boj,bjf->bfo/dot_general | solution.py:169
  (555 shorter events, 273.6 us)
Async XLA Ops:
  0.6 16.0 %copy-start.5 = (f32[512,128]{1,0:T(8,128)S(1)}, f32[512,128]{1,0:T(8,128)}, u32[]{:S(2)}) copy-start(f32[512,128]{1,0:T(8,128)} %param.16) | copy-start | bytes 786436
  1.5 19.2 %copy-start.7 = (f32[512,5,128]{2,0,1:T(8,128)S(1)}, f32[512,5,128]{2,0,1:T(8,128)}, u32[]{:S(2)}) copy-start(f32[512,5,128]{2,0,1:T(8,128)} %param.12) | copy-start | bytes 3932164
  8.5 73.6 %all-to-all-start.1 = ((s32[16,1,64]{2,1,0:T(1,128)}), s32[16,1,64]{2,1,0:T(1,128)}, u32[]{:S(2)}, u32[]{:S(2)}) async-start(s32[16,1,64]{2,1,0:T(1,128)} %and_select_fusion), calls=%async_computation.1 | async-start | bytes 16384 | tf_op jit(solution)/shard_map/all_to_all | solution.py:224
  20.8 8.3 copy-start.10
  27.0 6.2 copy-start.14
  59.3 4.0 copy-start.8
  59.5 0.6 copy-start.13
  60.5 10.9 %copy-start.1 = (f32[512,128]{1,0:T(8,128)}, f32[512,128]{1,0:T(8,128)S(1)}, u32[]{:S(2)}) copy-start(f32[512,128]{1,0:T(8,128)S(1)} %sub.416) | copy-start | bytes 786436
  63.3 9.8 %copy-start.15 = (s32[16]{0:T(128)S(1)}, s32[16]{0:T(128)}, u32[]{:S(2)}) copy-start(s32[16]{0:T(128)} %param.21) | copy-start | bytes 196
  63.4 9.8 %copy-start.3 = (f32[512,128]{1,0:T(8,128)S(1)}, f32[512,128]{1,0:T(8,128)}, u32[]{:S(2)}) copy-start(f32[512,128]{1,0:T(8,128)} %param.14) | copy-start | bytes 786436
  82.1 7.1 copy-start.6
  82.1 103.5 %all-to-all-start = ((f32[16,64,7,128]{3,1,2,0:T(8,128)}), f32[16,64,7,128]{3,1,2,0:T(8,128)}, u32[]{:S(2)}, u32[]{:S(2)}) async-start(f32[16,64,7,128]{3,1,2,0:T(8,128)} %copy.444), calls=%async_computation | async-start | bytes 7340032 | tf_op jit(solution)/shard_map/all_to_all | solution.py:222
  185.7 17.4 %all-to-all-start.2 = ((s32[16,64,128]{2,1,0:T(8,128)}), s32[16,64,128]{2,1,0:T(8,128)}, u32[]{:S(2)}, u32[]{:S(2)}) async-start(s32[16,64,128]{2,1,0:T(8,128)} %bitcast.13), calls=%async_computation.2 | async-start | bytes 1048576 | tf_op jit(solution)/shard_map/all_to_all | solution.py:223
  621.6 68.0 %copy-start.11 = (pred[256,256]{1,0:T(8,128)(4,1)S(1)}, pred[256,256]{1,0:T(8,128)(4,1)}, u32[]{:S(2)}) copy-start(pred[256,256]{1,0:T(8,128)(4,1)} %iota_compare_fusion.17) | copy-start | bytes 196612
  621.6 68.2 %copy-start.16 = (s32[2]{0:T(128)S(1)}, s32[2]{0:T(128)}, u32[]{:S(2)}) copy-start(s32[2]{0:T(128)} %iota_multiply_fusion) | copy-start | bytes 28
  621.8 205.0 %copy-start = (s32[512]{0:T(512)S(1)}, s32[512]{0:T(512)}, u32[]{:S(2)}) copy-start(s32[512]{0:T(512)} %param.19) | copy-start | bytes 6148
  737.0 106.4 %copy-start.12 = (f32[2,256]{1,0:T(2,128)}, f32[2,256]{1,0:T(2,128)S(1)}, u32[]{:S(2)}) copy-start(f32[2,256]{1,0:T(2,128)S(1)} %maximum_bitcast_fusion) | copy-start | bytes 6148
  737.0 7.0 collective-permute-start
  744.0 6.9 collective-permute-start.1
  750.9 6.9 collective-permute-start.2
  757.8 6.9 collective-permute-start.3
  764.7 6.9 collective-permute-start.4
  771.6 6.9 collective-permute-start.5
  778.5 6.9 collective-permute-start.6
  785.4 6.9 collective-permute-start.7
  792.3 6.9 collective-permute-start.8
  799.2 6.9 collective-permute-start.9
  806.1 6.9 collective-permute-start.10
  813.0 6.9 collective-permute-start.11
  819.9 6.9 collective-permute-start.12
  826.8 6.9 collective-permute-start.13
  833.7 6.9 collective-permute-start.14
  845.1 9.4 %copy-start.9 = (f32[512,4,128]{2,1,0:T(4,128)S(1)}, f32[512,4,128]{2,1,0:T(4,128)}, u32[]{:S(2)}) copy-start(f32[512,4,128]{2,1,0:T(4,128)} %param.13) | copy-start | bytes 3145732
  854.5 3.2 copy-start.2
  854.5 3.2 copy-start.4
